TPU v7x, 32 devices: a whole 2x2x4 slice. The times are simulated.
32 devices in a mesh: dp: 16 (over z, y, x), tensor: 2 (over core).
Axes of the slice: x: 2, y: 2, z: 4, core: 2. Of those that a mesh axis runs over, the one named last changes fastest.
Arguments:
- inputs: bfloat16 [32768, 768], P('dp'), may hold values from -6 to 6
- segments: int32 [32, 1024], P('dp'), may hold values from 0 to 7, never falling along the last dimension, each value on 1 to 512 neighbouring positions
- cotangent: bfloat16 [32768, 768], P('dp'), may hold values from -6 to 6
- weight_qkv: float32 [3, 768, 768], P(None, 'dp', 'tensor'), may hold values from -0.21875 to 0.21875
- first_qkv: float32 [3, 768, 768], P(None, 'dp', 'tensor'), may hold values from -64 to 64
- second_qkv: float32 [3, 768, 768], P(None, 'dp', 'tensor'), may hold values from 4.096 to 65.536
- weight_out: float32 [768, 768], P(('tensor', 'dp')), may hold values from -0.625 to 0.625
- first_out: float32 [768, 768], P(('tensor', 'dp')), may hold values from -24 to 24
- second_out: float32 [768, 768], P(('tensor', 'dp')), may hold values from 0.65536 to 10.48576
- weight_gate_up: float32 [2, 768, 3072], P(None, 'dp', 'tensor'), may hold values from -0.21875 to 0.21875
- first_gate_up: float32 [2, 768, 3072], P(None, 'dp', 'tensor'), may hold values from -24 to 24
- second_gate_up: float32 [2, 768, 3072], P(None, 'dp', 'tensor'), may hold values from 0.65536 to 10.48576
- weight_down: float32 [3072, 768], P(('tensor', 'dp')), may hold values from -0.109375 to 0.109375
- first_down: float32 [3072, 768], P(('tensor', 'dp')), may hold values from -56 to 56
- second_down: float32 [3072, 768], P(('tensor', 'dp')), may hold values from 3.2768 to 52.4288
- head_bias: float32 [2, 768], P(None, ('tensor', 'dp')), may hold values from -4 to 4
- first_head_bias: float32 [2, 768], P(None, ('tensor', 'dp')), may hold values from -64 to 64
- second_head_bias: float32 [2, 768], P(None, ('tensor', 'dp')), may hold values from 4.096 to 65.536
- norm_vectors: float32 [6, 768], P(None, 'dp'), may hold values from -1.5 to 1.75, as said below
- first_norm_vectors: float32 [6, 768], P(None, 'dp'), may hold values from -80 to 80
- second_norm_vectors: float32 [6, 768], P(None, 'dp'), may hold values from 8.192 to 131.072
Outputs:
- layer_out: bfloat16 [32768, 768], P('dp')
- input_grad: bfloat16 [32768, 768], P('dp')
- grad_qkv: float32 [3, 768, 768], P(None, 'dp', 'tensor')
- new_second_qkv: float32 [3, 768, 768], P(None, 'dp', 'tensor')
- new_weight_qkv: float32 [3, 768, 768], P(None, 'dp', 'tensor')
- grad_out: float32 [768, 768], P(('tensor', 'dp'))
- new_second_out: float32 [768, 768], P(('tensor', 'dp'))
- new_weight_out: float32 [768, 768], P(('tensor', 'dp'))
- grad_gate_up: float32 [2, 768, 3072], P(None, 'dp', 'tensor')
- new_second_gate_up: float32 [2, 768, 3072], P(None, 'dp', 'tensor')
- new_weight_gate_up: float32 [2, 768, 3072], P(None, 'dp', 'tensor')
- grad_down: float32 [3072, 768], P(('tensor', 'dp'))
- new_second_down: float32 [3072, 768], P(('tensor', 'dp'))
- new_weight_down: float32 [3072, 768], P(('tensor', 'dp'))
- grad_head_bias: float32 [2, 768], P(None, ('tensor', 'dp'))
- new_second_head_bias: float32 [2, 768], P(None, ('tensor', 'dp'))
- new_weight_head_bias: float32 [2, 768], P(None, ('tensor', 'dp'))
- grad_norm_vectors: float32 [6, 768], P(None, 'dp')
- new_second_norm_vectors: float32 [6, 768], P(None, 'dp')
- new_weight_norm_vectors: float32 [6, 768], P(None, 'dp')
Inputs may be any that keep to these rules, and one draw needn't show every extreme that they name: `segments`: each row numbers the documents packed into one sequence from 0 upward, never falling; a document has 1 to 512 tokens. `norm_vectors`: rows 2 and 4 lie in 0.25 to 1.75, the other rows in -1.5 to 1.5.
All inputs are finite; a program needn't handle non-finite values.
Results may differ from a plain program's by a relative error of at most 0.025.
Values may be sent and summed in bfloat16 or wider, within the bound.
A program may use at most 192 MiB of HBM per device.

v0:
```python
import functools
import math
import types

import jax
import jax.numpy as jnp
import numpy as np
from jax import lax
from jax.experimental import pallas as pl
from jax.experimental.pallas import tpu as pltpu
from jax.sharding import PartitionSpec as P

HEADS = 12
HEAD_DIM = 64
SEQ = 1024
STEP = 10

norm_epsilon = 1e-12
beta_first = 0.9
beta_second = 0.999
adam_epsilon = 1e-08
decay_rate = 0.1
matrix_rate = 0.05
vector_rate = 0.5

MESH = pl.DeviceIdType.MESH
TORUS = (4, 2, 2)
f32, bf16 = jnp.float32, jnp.bfloat16
LOG2E = 1.4426950408889634
FAR = 3e12
REACH = 512
BQ = 256
TM = 256
HC = 512
VMEM = pl.BlockSpec(memory_space=pltpu.VMEM)
SMEM = pl.BlockSpec(memory_space=pltpu.SMEM)
ANY = pl.BlockSpec(memory_space=pl.ANY)


def alibi_slopes(head_total):
    power_two = 2 ** int(math.floor(math.log2(head_total)))
    leading = [2.0 ** (-8.0 * (h + 1) / power_two) for h in range(power_two)]
    trailing = [
        2.0 ** (-8.0 * (2 * h + 1) / (2 * power_two)) for h in range(head_total - power_two)
    ]
    return np.array(leading + trailing, dtype=np.float32)


def place():
    me = lax.axis_index("dp")
    return lax.div(me, 4), lax.rem(lax.div(me, 2), 2), lax.rem(me, 2)


def chip(z, y, x):
    return z * 4 + y * 2 + x


def remote(src, dst, ssem, rsem, dp):
    return pltpu.make_async_remote_copy(
        src_ref=src,
        dst_ref=dst,
        send_sem=ssem,
        recv_sem=rsem,
        device_id={"dp": dp},
        device_id_type=MESH,
    )


def swap(src, dst, ssem, rsem):
    return pltpu.make_async_remote_copy(
        src_ref=src,
        dst_ref=dst,
        send_sem=ssem,
        recv_sem=rsem,
        device_id={"tensor": 1 - lax.axis_index("tensor")},
        device_id_type=MESH,
    )


def greet(chips, core):
    barrier = pltpu.get_barrier_semaphore()
    count = 0
    if chips:
        z, y, x = place()
        peers = [chip(lax.rem(z + d, 4), y, x) for d in (1, 2, 3)]
        for dp in peers + [chip(z, 1 - y, x), chip(z, y, 1 - x)]:
            pl.semaphore_signal(barrier, inc=1, device_id={"dp": dp}, device_id_type=MESH)
            count += 1
    if core:
        other = {"tensor": 1 - lax.axis_index("tensor")}
        pl.semaphore_signal(barrier, inc=1, device_id=other, device_id_type=MESH)
        count += 1
    pl.semaphore_wait(barrier, count)


class Gather:
    def __init__(self, src, dst, first, ssem, rsem, lsem):
        self.src, self.dst, self.first = src, dst, first
        self.ssem, self.rsem, self.lsem = ssem, rsem, lsem
        self.z, self.y, self.x = place()

    def own(self):
        return pltpu.make_async_copy(self.src, self.dst(self.z, self.y, self.x), self.lsem)

    def along_z(self, d, arriving):
        z, y, x = self.z, self.y, self.x
        other = lax.rem(z + (4 - d if arriving else d), 4)
        slot = self.dst(other if arriving else z, y, x)
        return remote(self.src, slot, self.ssem.at[d - 1], self.rsem.at[d - 1], chip(other, y, x))

    def plane(self, k, arriving):
        z, y, x = self.z, self.y, self.x
        whole = slice(None)
        on_x = (self.first == "x") == (k == 0)
        dp = chip(z, y, 1 - x) if on_x else chip(z, 1 - y, x)
        yy, xx = y, x
        if arriving:
            yy, xx = (y, 1 - x) if on_x else (1 - y, x)
        if k == 1:
            yy, xx = (whole, xx) if on_x else (yy, whole)
        part = self.dst(whole, yy, xx)
        return remote(part, part, self.ssem.at[3 + k], self.rsem.at[3 + k], dp)

    def s0(self):
        self.own().start()
        for d in (1, 3, 2):
            self.along_z(d, False).start()

    def s1(self):
        self.own().wait()
        for d in (1, 3, 2):
            self.along_z(d, False).wait_send()
            self.along_z(d, True).wait_recv()
        self.plane(0, False).start()

    def s2(self):
        self.plane(0, False).wait_send()
        self.plane(0, True).wait_recv()
        self.plane(1, False).start()

    def s3(self):
        self.plane(1, False).wait_send()
        self.plane(1, True).wait_recv()


class GatherLate(Gather):
    def hop(self, k, arriving):
        z, y, x = self.z, self.y, self.x
        whole = slice(None)
        on_x = (self.first == "x") == (k == 0)
        dp = chip(z, y, 1 - x) if on_x else chip(z, 1 - y, x)
        yy, xx = y, x
        if arriving:
            yy, xx = (y, 1 - x) if on_x else (1 - y, x)
        if k == 1:
            yy, xx = (whole, xx) if on_x else (yy, whole)
        part = self.dst(z, yy, xx)
        src = self.src if k == 0 and not arriving else part
        return remote(src, part, self.ssem.at[3 + k], self.rsem.at[3 + k], dp)

    def along_z(self, d, arriving):
        whole = slice(None)
        other = lax.rem(self.z + (4 - d if arriving else d), 4)
        part = self.dst(other if arriving else self.z, whole, whole)
        dp = chip(other, self.y, self.x)
        return remote(part, part, self.ssem.at[d - 1], self.rsem.at[d - 1], dp)

    def s0(self):
        self.own().start()
        self.hop(0, False).start()

    def s1(self):
        self.own().wait()
        self.hop(0, False).wait_send()
        self.hop(0, True).wait_recv()
        self.hop(1, False).start()

    def s2(self):
        self.hop(1, False).wait_send()
        self.hop(1, True).wait_recv()
        for d in (1, 3, 2):
            self.along_z(d, False).start()

    def s3(self):
        for d in (1, 3, 2):
            self.along_z(d, False).wait_send()
            self.along_z(d, True).wait_recv()


class Scatter:
    def __init__(self, g, r1, r2, r3, out, first, ssem, rsem):
        self.r1, self.r2, self.r3, self.out, self.ssem, self.rsem = r1, r2, r3, out, ssem, rsem
        z, y, x = self.z, self.y, self.x = place()
        on_y, on_x = chip(z, 1 - y, x), chip(z, y, 1 - x)
        if first == "y":
            self.block = lambda zz, a, b: g(zz, a, b)
            self.a, self.b, self.to1, self.to2 = y, x, on_y, on_x
        else:
            self.block = lambda zz, a, b: g(zz, b, a)
            self.a, self.b, self.to1, self.to2 = x, y, on_x, on_y

    def c1(self):
        whole = slice(None)
        src = self.block(whole, 1 - self.a, whole)
        return remote(src, self.r1, self.ssem.at[0], self.rsem.at[0], self.to1)

    def c2(self):
        src = self.r1.at[:, 1 - self.b]
        return remote(src, self.r2, self.ssem.at[1], self.rsem.at[1], self.to2)

    def c3(self, d):
        to = lax.rem(self.z + d, 4)
        dp = chip(to, self.y, self.x)
        return remote(
            self.r2.at[to], self.r3.at[d - 1], self.ssem.at[1 + d], self.rsem.at[1 + d], dp
        )

    def s0(self):
        self.c1().start()

    def s1(self):
        self.c1().wait()
        o = 1 - self.b

        def add(zz, carry):
            t = self.r1.at[zz, o]
            t[...] = (t[...].astype(f32) + self.block(zz, self.a, o)[...].astype(f32)).astype(t.dtype)
            return carry

        lax.fori_loop(0, 4, add, 0)
        self.c2().start()

    def s2(self):
        self.c2().wait()

        def add(d, carry):
            zz = lax.rem(self.z + d, 4)
            t = self.r2.at[zz]
            here = self.r1[zz, self.b].astype(f32) + self.block(zz, self.a, self.b)[...].astype(f32)
            t[...] = (t[...].astype(f32) + here).astype(t.dtype)
            return carry

        lax.fori_loop(1, 4, add, 0)
        for d in (2, 1, 3):
            self.c3(d).start()

    def s3(self):
        for d in (2, 1, 3):
            self.c3(d).wait()
        z = self.z
        total = self.block(z, self.a, self.b)[...].astype(f32) + self.r1[z, self.b].astype(f32)
        total = total + self.r2[z].astype(f32)
        for d in range(3):
            total = total + self.r3[d].astype(f32)
        self.out[...] = total


def run(flows, stage):
    for flow in flows:
        getattr(flow, f"s{stage}")()


def routed():
    return lax.axis_size("dp") == TORUS[0] * TORUS[1] * TORUS[2]


def nt(a, b):
    return lax.dot_general(a, b, (((1,), (1,)), ((), ())), preferred_element_type=f32)


def tn(a, b):
    return lax.dot_general(a, b, (((0,), (0,)), ((), ())), preferred_element_type=f32)


def nn(a, b):
    return jnp.dot(a, b, preferred_element_type=f32)


def span(b, seq):
    lo = max(0, (b * BQ - REACH + 1) // BQ * BQ)
    hi = min(seq, -(-(b * BQ + BQ - 1 + REACH) // BQ) * BQ)
    return lo, hi


def half(value, which):
    lane = lax.broadcasted_iota(jnp.int32, value.shape, 1)
    keep = (lane < 64) if which == 0 else (lane >= 64)
    return jnp.where(keep, value, jnp.zeros_like(value))


def stats(h):
    c = h - jnp.mean(h, axis=-1, keepdims=True)
    return c, spread(c)


def spread(c):
    return lax.rsqrt(jnp.mean(c * c, axis=-1, keepdims=True) + norm_epsilon)


def norm_back(e, n, r):
    return r * (e - jnp.mean(e, axis=-1, keepdims=True) - n * jnp.mean(e * n, axis=-1, keepdims=True))


class Rows:
    def __init__(self, ref, lane, lanes):
        self.ref, self.lane, self.lanes = ref, lane, lanes

    def cols(self, pair):
        return pl.ds(pl.multiple_of(self.lane + pair * 384, 128), 128)

    def tile(self, i):
        return self.ref.at[lax.div(i, 2), lax.rem(i, 2), :, self.lane : self.lane + self.lanes]

    def block(self, s, b, pair):
        return self.ref.at[2 * s + b // 2, b % 2, :, self.cols(pair)]

    def span(self, s, lo, hi, pair):
        parts = [self.block(s, b, pair)[...] for b in range(lo // TM, hi // TM)]
        return jnp.concatenate(parts, axis=0)

    def all(self):
        v = self.ref[:, :, :, self.lane : self.lane + self.lanes]
        return v.reshape(-1, self.lanes)


class Far:
    def __init__(self, ref, seq):
        self.ref, self.seq = ref, seq
        self.across = ref.shape[1] // BQ

    def at(self, lo, hi, b):
        row, col = b // self.across * self.seq, b % self.across * BQ
        return self.ref.at[row + lo : row + hi, col : col + BQ]

    def fill(self, seg_ref, s):
        seq = self.seq
        segs = seg_ref[pl.ds(s, 1), :].astype(f32)
        for c in range(seq // 128):
            mine = jnp.broadcast_to(segs[:, c * 128 : (c + 1) * 128], (128, 128)).T
            for b in range(seq // BQ):
                r = lax.broadcasted_iota(jnp.int32, (128, BQ), 0) + c * 128
                k = lax.broadcasted_iota(jnp.int32, (128, BQ), 1) + b * BQ
                d = jnp.abs(r - k).astype(f32)
                same = jnp.concatenate([mine] * (BQ // 128), axis=1) == segs[:, b * BQ : (b + 1) * BQ]
                self.at(c * 128, (c + 1) * 128, b)[...] = jnp.where(same, d, FAR)


def attend(s, pair, q, k, v, vt_ref, far, slopes, ctx_ref, lse_ref, seq, pairs):
    cols = pl.ds(pl.multiple_of(pair * 128, 128), 128)
    vt_ref[...] = v.span(s, 0, seq, pair).T
    for b in range(seq // BQ):
        lo, hi = span(b, seq)
        qb = q.block(s, b, pair)[...] * jnp.asarray(HEAD_DIM**-0.5, bf16)
        kb = k.span(s, lo, hi, pair)
        score = [nt(kb, half(qb, h)) * LOG2E - slopes[h] * far.at(lo, hi, b)[...] for h in range(2)]
        top = [jnp.max(t, axis=0, keepdims=True) for t in score]
        weight = [jnp.exp2(t - m) for t, m in zip(score, top)]
        total = [jnp.sum(e, axis=0, keepdims=True) for e in weight]
        out = [
            nn(vt_ref[64 * h : 64 * h + 64, lo:hi], weight[h].astype(bf16)) * (1.0 / total[h])
            for h in range(2)
        ]
        for h in range(2):
            lse_ref[s * pairs + pair, h : h + 1, b * BQ : (b + 1) * BQ] = top[h] + jnp.log2(total[h])
        at = pl.ds(pl.multiple_of(s * seq + b * BQ, BQ), BQ)
        ctx_ref[at, cols] = jnp.concatenate(out, axis=0).T.astype(bf16)


def attend_back(
    s, pair, q, k, v, ctx_ref, dctx_ref, lse_ref, far, slopes, kt_ref, dk_acc, dv_acc, dq, dk, dv, seq, pairs
):
    cols = pl.ds(pl.multiple_of(pair * 128, 128), 128)
    kt_ref[...] = k.span(s, 0, seq, pair).T
    dk_acc[...] = jnp.zeros(dk_acc.shape, f32)
    dv_acc[...] = jnp.zeros(dv_acc.shape, f32)
    for b in range(seq // BQ):
        lo, hi = span(b, seq)
        at = pl.ds(pl.multiple_of(s * seq + b * BQ, BQ), BQ)
        qb = q.block(s, b, pair)[...] * jnp.asarray(HEAD_DIM**-0.5, bf16)
        kb, vb = k.span(s, lo, hi, pair), v.span(s, lo, hi, pair)
        db = dctx_ref[at, cols]
        prod = (db.astype(f32) * ctx_ref[at, cols].astype(f32)).T
        out = []
        for h in range(2):
            qh, dh = half(qb, h), half(db, h)
            delta = jnp.sum(prod[64 * h : 64 * h + 64], axis=0, keepdims=True)
            lse = lse_ref[s * pairs + pair, h : h + 1, b * BQ : (b + 1) * BQ]
            p = jnp.exp2(nt(kb, qh) * LOG2E - slopes[h] * far.at(lo, hi, b)[...] - lse)
            ds = (p * (nt(vb, dh) - delta)).astype(bf16)
            dv_acc[lo:hi, :] += nn(p.astype(bf16), dh)
            dk_acc[lo:hi, :] += nn(ds, qh)
            out.append(nn(kt_ref[64 * h : 64 * h + 64, lo:hi], ds))
        dq_val = jnp.concatenate(out, axis=0).T * HEAD_DIM**-0.5
        dq.block(s, b, pair)[...] = dq_val.astype(bf16)
    for b in range(seq // BQ):
        dk.block(s, b, pair)[...] = dk_acc[b * BQ : (b + 1) * BQ, :].astype(bf16)
        dv.block(s, b, pair)[...] = dv_acc[b * BQ : (b + 1) * BQ, :].astype(bf16)


AG = (
    (10, 0, 11, 20, 80, 1, 21, 30, 2, 12, 40, 3, 22, 31),
    (81, 50),
    (32, 41),
    (13, 60),
    (51, 42),
    (82, 23),
    (61, 70),
    (52, 62),
    (),
    (33,),
    (53, 83, 71, 43, 63),
    (72,),
    (),
    (73,),
)
RS = (
    (),
    (),
    (1, 11),
    (2, 20),
    (),
    (12,),
    (30,),
    (21, 31),
    (32,),
    (50, 40, 22),
    (51,),
    (41, 52),
    (60, 33),
    (42,),
    (61, 3, 23, 13, 62),
    (63, 43, 53),
)


def layer_kernel(names, seq, pairs, routes, lead, *refs):
    R = types.SimpleNamespace(**dict(zip(names, refs)))
    seg_ref, slope_ref, x_hbm, cot_hbm = R.seg, R.slope, R.x, R.cot
    out_hbm, dx_hbm, keep_hbm = R.out, R.dx, R.keep
    wq, wg, wu, wd, wo5 = R.wq, R.wg, R.wu, R.wd, R.wo5
    wo, sm, vec, dvec, gd = R.wo, R.sm, R.vec, R.dvec, R.gd
    io, s1, q1, s2, q2, n1 = R.io, R.s1, R.q1, R.s2, R.q2, R.n1
    hv, av, bv, ctx, lse, vt = R.hv, R.av, R.bv, R.ctx, R.lse, R.vt
    io_sem, out_sem, dx_sem = R.io_sem, R.out_sem, R.dx_sem
    xs, xr, misc = R.xs, R.xr, R.misc
    rows, model = io.shape
    width, ff = ctx.shape[1], av.shape[3]
    tiles, nb = rows // TM, lead[0] * lead[1] * lead[2]
    each, each_out, each_ff = model // nb, width // nb, ff // nb
    pad_out = wo5.shape[3]
    count = seg_ref.shape[0]
    HC = ff // 2
    at = lambda i: pl.ds(pl.multiple_of(i * TM, TM), TM)
    tile = lambda ref, i: ref.at[lax.div(i, 2), lax.rem(i, 2)]
    load = lambda hbm, i: pltpu.make_async_copy(hbm.at[at(i)], io.at[at(i)], io_sem.at[i])
    emit = lambda i: pltpu.make_async_copy(io.at[at(i)], out_hbm.at[at(i)], out_sem.at[i])
    exch = lambda k, i: swap((s1, s2, s1, s1)[k].at[at(i)], (q1, q2, q1, q1)[k].at[at(i)], xs.at[k, i], xr.at[k, i])
    me = lax.axis_index("dp")
    core = lax.axis_index("tensor")
    head0 = core * (2 * pairs)
    slopes_of = lambda pair: [slope_ref[head0 + 2 * pair + h] for h in range(2)]
    gate_w = lambda ref, c: ref[:, :, :, :, c : c + HC].reshape(model, HC)
    lh = lead[0] // 2

    def down_w(c):
        if routes:
            return wd[c // HC * lh : (c // HC + 1) * lh].reshape(HC, model)
        return wd[0, 0, 0, c : c + HC, :]

    def each_tile(f, lo, hi):
        def body(i, carry):
            f(i)
            return carry

        lax.fori_loop(lo, hi, body, 0)

    each_tile(lambda i: load(x_hbm, i).start(), 0, tiles)

    if routes:
        lanes = n1.shape[1]
        place_of, moves, row = {}, [], 0

        def stage_in(name, src):
            nonlocal row
            r, c = src.shape
            place_of[name] = []
            for a in range(0, c, lanes):
                w = min(lanes, c - a)
                spot_in = n1.at[row : row + r, 0:w]
                cp = pltpu.make_async_copy(src.at[:, a : a + w], spot_in, misc.at[len(moves)])
                cp.start()
                moves.append(cp)
                place_of[name].append(spot_in)
                row += -(-r // 8) * 8

        for j in range(3):
            stage_in(j, R.weight_qkv.at[j])
        for j in range(2):
            stage_in(3 + j, R.weight_gate_up.at[j])
        stage_in(5, R.weight_down)
        stage_in(6, R.weight_out)
        for cp in moves:
            cp.wait()
        fetch = lambda name: jnp.concatenate([p[...] for p in place_of[name]], axis=1)
        for j in range(3):
            mine = fetch(j).astype(bf16)
            for p in range(pairs):
                R.qkv_src[p * each : (p + 1) * each, j * 128 : (j + 1) * 128] = mine[:, p * 128 : (p + 1) * 128]
        R.gate_src[...] = fetch(3).astype(bf16)
        R.up_src[...] = fetch(4).astype(bf16)
        R.down_src[...] = fetch(5).astype(bf16)
        pad = R.out_src.shape[0] - each_out
        R.out_src[...] = jnp.concatenate(
            [fetch(6), jnp.zeros((pad, model), f32)], axis=0
        ).astype(bf16)
        spot = R.spot
        spot[...] = jnp.zeros(spot.shape, f32)
        spot[0:6, 0:each] = R.norm_vectors[...]
        spot[6:8, 0:each_out] = R.head_bias[...]
        R.small_src[...] = spot[...].astype(bf16)
        gs, gr, gl = R.gs, R.gr, R.gl
        flows = []

        def flow(src, dst, cuts, kind=Gather):
            made = []
            for a, b, first in cuts:
                j = len(flows)
                slot = lambda z, y, x, a=a, b=b: dst.at[z, y, x, a:b]
                made.append(kind(src.at[a:b], slot, first, gs.at[j], gr.at[j], gl.at[j]))
                flows.append(made[-1])
            return made

        both = lambda a, m, b: ((a, m, "x"), (m, b, "y"))
        gate_up = lambda a, b: flow(R.gate_src, wg, ((a, b, "x"),)) + flow(R.up_src, wu, ((a, b, "y"),))
        qkv_src, down_src = R.qkv_src, R.down_src
        cut = each // 3
        pieces = [
            flow(qkv_src, wq, both(0, 16, each)) + flow(R.small_src, sm, ((0, 16, "x"),)),
            flow(qkv_src, wq, both(each, 80, 2 * each)),
            flow(qkv_src, wq, both(2 * each, 112, 3 * each)),
            flow(R.out_src, wo5, both(0, 16, pad_out)),
            gate_up(0, cut),
            gate_up(cut, 2 * cut),
            gate_up(2 * cut, each),
            flow(down_src, wd, both(0, 32, 64)),
            flow(down_src, wd, both(64, 80, each_ff), GatherLate),
        ]

        def bring(*steps):
            for step in steps:
                run(pieces[step // 10], step % 10)

        greet(True, True)
        bring(*AG[0])
    else:
        pairs_in = [
            (R.weight_qkv, wq), (R.weight_gate, wg), (R.weight_up, wu),
            (R.weight_down, wd), (R.weight_out, wo5), (R.small, sm),
        ]
        copies = [pltpu.make_async_copy(a, b.at[0, 0, 0], misc.at[2 + j]) for j, (a, b) in enumerate(pairs_in)]
        for cp in copies:
            cp.start()
        greet(False, True)
        for cp in copies:
            cp.wait()
    if routes:
        wide_zero = jnp.zeros((8, model - 128), f32)
        lane = lax.broadcasted_iota(jnp.int32, (8, 128), 1)
        row = lax.broadcasted_iota(jnp.int32, (8, 128), 0)
        width_of = jnp.where(row < 6, each, each_out)
        upper, lower = 0.0, 0.0
        for b in range(nb):
            piece = sm[b // 4, (b // 2) % 2, b % 2].astype(f32)[0:8]
            piece = jnp.concatenate([jnp.where(lane < width_of, piece, 0.0), wide_zero], axis=1)
            upper = upper + pltpu.roll(piece, b * each, 1)
            lower = lower + pltpu.roll(piece, b * each_out, 1)
        vec[0:8, :], vec[8:16, :] = upper, lower
    else:
        vec[0:8, :] = sm[0, 0, 0, 0:16, :].astype(f32)[0:8]
        vec[8:16, :] = vec[0:8, :]
    bo, bd, g1, c1, g2, c2 = (vec[k : k + 1, :] for k in range(6))

    pair_w = lambda p: wq[:, :, :, p * each : (p + 1) * each, :].reshape(model, 3 * 128)
    qkv = [Rows(bv, j * 128, 128) for j in range(3)]
    keep = lambda out: pltpu.make_async_copy(
        *((bv.at[:, :, :, 0 : 3 * width], keep_hbm) if out else (keep_hbm, bv.at[:, :, :, 0 : 3 * width])),
        misc.at[0],
    )
    each_tile(lambda i: load(x_hbm, i).wait(), 0, tiles)
    far = Far(n1, seq)

    def project(p):
        here = slice(p * 128, (p + 1) * 128)
        bias = jnp.concatenate([vec[14:15, here], jnp.zeros((1, 128), f32), vec[15:16, here]], axis=1)

        def tile_of(i):
            Rows(bv, p * 384, 384).tile(i)[...] = (nn(io[at(i), :], pair_w(p)) + bias).astype(bf16)

        each_tile(tile_of, 0, tiles)
        if routes:
            bring(*AG[1 + 3 * p])

    def forward(it):
        pair, turn = lax.div(it, count), lax.rem(it, count)
        far.fill(seg_ref, turn)
        attend(turn, pair, *qkv, vt, far, slopes_of(pair), ctx, lse, seq, pairs)
        for p in range(pairs):

            @pl.when(it == p * count + count - 2)
            def _(p=p):
                if routes:
                    bring(*AG[2 + 3 * p])

            @pl.when(it == p * count + count - 1)
            def _(p=p):
                if routes:
                    bring(*AG[3 + 3 * p])
                if p + 1 < pairs:
                    project(p + 1)

    project(0)
    each_tile(forward, 0, count * pairs)
    keep(True).start()
    wo[...] = wo5[:, :, :, :each_out, :].astype(f32).reshape(width, model).astype(bf16)

    def phase_a(i):
        s1[at(i), :] = nn(ctx[at(i), :], wo[...]).astype(bf16)
        exch(0, i).start()

    each_tile(phase_a, 0, tiles)
    keep(True).wait()

    if routes:
        lo_hi = (slice(0, lh), slice(lh, lead[0]))
        stage = [gd.at[part, :, :, 0 : TM * 2 // nb, :] for part in lo_hi]
    else:
        stage = [gd.at[:, :, :, j * TM : (j + 1) * TM, :] for j in range(2)]

    def meet_one(i):
        exch(0, i).wait()

    def norm_one(i, parity):
        attn = s1[at(i), :].astype(f32) + q1[at(i), :].astype(f32) + bo
        c, r = stats(io[at(i), :].astype(f32) + attn)
        n1[at(i), :] = c
        stage[parity][...] = (c * r * g1 + c1).astype(bf16).reshape(stage[parity].shape)

    def geglu(i, parity):
        xb = stage[parity][...].reshape(TM, model)
        for c in range(0, ff, HC):
            gate, up = nn(xb, gate_w(wg, c)), nn(xb, gate_w(wu, c))
            cdf = 0.5 * (1.0 + lax.erf(gate * 0.7071067811865476))
            gel = gate * cdf
            slope = cdf + gate * (jnp.exp(gate * gate * -0.5) * 0.3989422804014327)
            tile(hv, i)[:, c : c + HC] = (gel * up).astype(bf16)
            tile(av, i)[:, c : c + HC] = (up * slope).astype(bf16)
            tile(bv, i)[:, c : c + HC] = gel.astype(bf16)

    def phase_b(j):
        meet_one(2 * j + 1)
        meet_one(2 * j + 2)
        norm_one(2 * j + 1, 1)
        geglu(2 * j, 0)
        norm_one(2 * j + 2, 0)
        geglu(2 * j + 1, 1)
        for i in (2 * j + 1, 2 * j + 2):
            load(cot_hbm, i).start()

    meet_one(0)
    norm_one(0, 0)
    load(cot_hbm, 0).start()
    if routes:
        bring(*AG[10])
    each_tile(phase_b, 0, 1)
    if routes:
        bring(*AG[11])
    each_tile(phase_b, 1, 2)
    if routes:
        bring(*AG[12])
    each_tile(phase_b, 2, tiles // 2 - 1)
    meet_one(tiles - 1)
    norm_one(tiles - 1, 1)
    load(cot_hbm, tiles - 1).start()
    geglu(tiles - 2, 0)
    geglu(tiles - 1, 1)
    if routes:
        bring(*AG[13])

    dvec[...] = jnp.zeros(dvec.shape, f32)

    def meet_two(i):
        exch(1, i).wait()
        load(cot_hbm, i).wait()

    def norm_two(i):
        c = n1[at(i), :]
        x1 = c * spread(c) * g1 + c1
        ffn = s2[at(i), :].astype(f32) + q2[at(i), :].astype(f32) + bd
        h, r2 = stats(x1 + ffn)
        n2 = h * r2
        dy = io[at(i), :].astype(f32)
        io[at(i), :] = (n2 * g2 + c2).astype(bf16)
        dvec[4:5, :] += jnp.sum(dy * n2, axis=0, keepdims=True)
        dvec[5:6, :] += jnp.sum(dy, axis=0, keepdims=True)
        dh2 = norm_back(dy * g2, n2, r2)
        dvec[1:2, :] += jnp.sum(dh2, axis=0, keepdims=True)
        s2[at(i), :] = dh2.astype(bf16)
        q2[at(i), :] = x1.astype(bf16)

    def down(i):
        s2[at(i), :] = nn(tile(hv, i)[...], wd[...].reshape(ff, model)).astype(bf16)

    def phase_down(i):
        down(i)
        exch(1, i).start()

    def phase_norm(i):
        meet_two(i)
        norm_two(i)
        emit(i).start()

    lag = 3

    def phase_c(i):
        meet_two(i - lag)
        norm_two(i - lag)
        down(i)
        emit(i - lag).start()
        exch(1, i).start()

    each_tile(phase_down, 0, lag)
    each_tile(phase_c, lag, tiles)
    each_tile(phase_norm, tiles - lag, tiles)

    quarter = ff // 4

    def grad_down(c):
        cols = pl.ds(pl.multiple_of(c * quarter, 128), quarter)
        val = tn(hv[:, :, :, cols].reshape(rows, quarter), s2[...]).astype(bf16)
        if routes:
            gd[c] = val.reshape(gd.shape[1:])
        else:
            gd[0, 0, 0, pl.ds(pl.multiple_of(c * quarter, 128), quarter), :] = val

    each_tile(grad_down, 0, 4)
    if routes:
        z, y, x = place()
        peers = [chip(lax.rem(z + d, 4), y, x) for d in (1, 2, 3)]
        peers += [chip(z, 1 - y, x), chip(z, y, 1 - x)]
        other = {"tensor": 1 - core}

        def ready(sem, devices):
            for dev in devices:
                pl.semaphore_signal(sem, inc=1, device_id=dev, device_id_type=MESH)
            pl.semaphore_wait(sem, len(devices))

        ss, sr = R.ss, R.sr
        sent = []

        def back_flow(g, r1, r2, r3, out, cuts, lo=0, lanes=None, shift=(0, 0)):
            made = []
            hi = lo + (lanes or out.shape[1])
            down, along = shift
            for a, b, first in cuts:
                j = len(sent)
                made.append(
                    Scatter(
                        lambda z, y, x, a=a, b=b: g.at[z, y, x, a - down : b - down, lo + along : hi + along],
                        r1(a, b), r2(a, b), r3(a, b), out.at[a:b, lo:hi], first, ss.at[j], sr.at[j],
                    )
                )
                sent.append(made[-1])
            return made

        def spare(top, deep, left, right):
            return (
                lambda a, b: hv.at[:, :, top + a : top + b, left[0] : left[1]],
                lambda a, b: hv.at[:, 0, deep + a : deep + b, right[0] : right[1]],
                lambda a, b: hv.at[0:3, 1, deep + a : deep + b, right[0] : right[1]],
            )

        own = lambda r1, r2, r3: (
            lambda a, b: r1.at[:, :, a:b],
            lambda a, b: r2.at[:, a:b],
            lambda a, b: r3.at[:, a:b],
        )
        eff = wd.shape[3]
        downs = back_flow(
            gd,
            lambda a, b: hv.at[:, :, a:b, 0:model],
            lambda a, b: hv.at[:, 0, eff + a : eff + b, 0:model],
            lambda a, b: hv.at[0:3, 1, eff + a : eff + b, 0:model],
            R.g_down,
            both(0, 48, eff),
        )
        def wide(g, j, out, first, lo, top, end):
            lanes = slice(lo, lo + HC)
            return back_flow(
                g,
                lambda a, b: av.at[:, :, j * each + a : j * each + b, lanes],
                lambda a, b: av.at[:, j, 2 * each + a : 2 * each + b, lanes],
                lambda a, b: av.at[0:3, j, 3 * each + a : 3 * each + b, lanes],
                out,
                ((top, end, first),),
                lo,
                HC,
            )

        gates = [
            wide(wg, 0, R.g_gate, "x", lo, 0, each) + wide(wu, 1, R.g_up, "y", lo, 0, each)
            for lo in (0, HC)
        ]
        outs_flow = back_flow(wo5, *spare(2 * eff, 2 * eff + pad_out, (0, model), (0, model)), R.g_out, both(0, 16, pad_out))
        heads_flow = [
            back_flow(
                wd,
                *spare(0, 0, (model, model + width), (model + width, model + 2 * width)),
                R.g_qkv,
                both(p * each, p * each + (32 if p == 1 else 16), (p + 1) * each),
                shift=((p - p % 2) * each, p // 2 * width),
            )
            for p in range(pairs)
        ]
        heads_flow[-1] += back_flow(R.gsm, *own(R.rs1, R.rs2, R.rs3), R.g_small, ((0, 8, "x"),))
        parts = [downs, gates[0], gates[1], outs_flow, *heads_flow]

        def push(*steps):
            for step in steps:
                run(parts[step // 10], step % 10)

        chips = [{"dp": p} for p in peers]

    def ffn_back(c, i):
        df = s2[at(i), :]
        dh = nt(df, down_w(c))
        a, b = tile(av, i), tile(bv, i)
        dg = (dh * a[:, c : c + HC].astype(f32)).astype(bf16)
        du = (dh * b[:, c : c + HC].astype(f32)).astype(bf16)
        a[:, c : c + HC] = dg
        b[:, c : c + HC] = du
        part = nt(dg, gate_w(wg, c)) + nt(du, gate_w(wu, c))
        if c > 0:
            part = part + s1[at(i), :].astype(f32)
        s1[at(i), :] = part.astype(bf16)
        if c + HC == ff:
            exch(2, i).start()

    def meet_back(i):
        exch(2, i).wait()
        emit(i).wait()

    def norm_one_back(i):
        c = n1[at(i), :]
        r = spread(c)
        n = c * r
        dx1 = s2[at(i), :].astype(f32) + (s1[at(i), :].astype(f32) + q1[at(i), :].astype(f32))
        dvec[2:3, :] += jnp.sum(dx1 * n, axis=0, keepdims=True)
        dvec[3:4, :] += jnp.sum(dx1, axis=0, keepdims=True)
        dh1 = norm_back(dx1 * g1, n, r)
        dvec[0:1, :] += jnp.sum(dh1, axis=0, keepdims=True)
        da = dh1.astype(bf16)
        io[at(i), :] = da
        s2[at(i), 0:width] = nt(da, wo[...]).astype(bf16)

    def grad_wide(c):
        cols = pl.ds(pl.multiple_of(c * 256, 256), 256)
        for src, dst in ((av, wg), (bv, wu)):
            val = tn(q2[...], src[:, :, :, cols].reshape(rows, 256)).astype(bf16)
            dst[:, :, :, :, cols] = val.reshape(dst.shape[:4] + (256,))

    per = HC // 256
    if routes:
        ready(R.ready.at[0], chips)
        push(0)
    mid = tiles // 2
    each_tile(lambda i: ffn_back(0, i), 0, tiles)
    if routes:
        push(*RS[0])
    each_tile(grad_wide, 0, per)
    if routes:
        ready(R.ready.at[1], chips)
        push(10, *RS[1])
    each_tile(lambda i: ffn_back(HC, i), 0, tiles)
    if routes:
        push(*RS[2])

    def phase_e(j):
        meet_back(2 * j)
        meet_back(2 * j + 1)
        norm_one_back(2 * j)
        norm_one_back(2 * j + 1)
        grad_wide(per + j)

    each_tile(phase_e, 0, per)

    def phase_last(i):
        meet_back(i)
        norm_one_back(i)

    each_tile(phase_last, 2 * per, tiles)
    keep(False).start()
    reload = pltpu.make_async_copy(x_hbm, q2, misc.at[1])
    reload.start()
    dwo = tn(ctx[...], io[...])
    wo5[:, :, :, :each_out, :] = dwo.reshape(lead + (each_out, model)).astype(bf16)
    if routes:
        ready(R.ready.at[2], chips + [other])
        push(*RS[3])
    else:
        pl.semaphore_signal(R.ready.at[2], inc=1, device_id={"tensor": 1 - core}, device_id_type=MESH)
        pl.semaphore_wait(R.ready.at[2], 1)
        grads_out = [(wg, R.g_gate), (wu, R.g_up), (gd, R.g_down), (wo5, R.g_out)]
        copies = [pltpu.make_async_copy(a.at[0, 0, 0], b, misc.at[2 + j]) for j, (a, b) in enumerate(grads_out)]
        for cp in copies:
            cp.start()
    keep(False).wait()

    d_pairs = [Rows(bv, p * 384, 384) for p in range(pairs)]
    dk_acc, dv_acc = (n1.at[seq : 2 * seq, j : j + 128] for j in (BQ, BQ + 128))
    reload.wait()

    def at_pair(pair, tables, first):
        for p in range(pairs):

            @pl.when(pair == p)
            def _(p=p):
                push(*tables[first + 3 * p])

    def backward(pair):
        def one(turn):
            far.fill(seg_ref, turn)
            attend_back(
                turn, pair, *qkv, ctx, s2, lse, far, slopes_of(pair), vt, dk_acc, dv_acc, *qkv, seq, pairs
            )

        each_tile(one, 0, count - 1)
        if routes:
            at_pair(pair, RS, 4)
        each_tile(one, count - 1, count)
        if routes:
            at_pair(pair, RS, 5)
        cols = pl.ds(pl.multiple_of(pair * 384, 128), 384)
        val = tn(q2[...], bv[:, :, :, cols].reshape(rows, 384)).astype(bf16).reshape(lead + (each, 384))
        for p in range(pairs):

            @pl.when(pair == p)
            def _(p=p):
                wd[:, :, :, p % 2 * each : (p % 2 + 1) * each, p // 2 * width : (p // 2 + 1) * width] = val
                if routes and p < pairs - 1:
                    push(*RS[6 + 3 * p])

    each_tile(backward, 0, pairs)

    def add_tile(d, i, total):
        return total + jnp.sum(d.tile(i)[...].astype(f32), axis=0, keepdims=True)

    totals = [
        lax.fori_loop(0, tiles, functools.partial(add_tile, d), jnp.zeros((1, 384), f32)) for d in d_pairs
    ]
    rows_of = [jnp.concatenate([t[:, j : j + 128] for t in totals], axis=1) for j in (0, 256)]
    heads = jnp.concatenate([jnp.zeros((6, width), f32)] + rows_of, axis=0)
    if routes:
        row = lax.broadcasted_iota(jnp.int32, (8, 128), 0)
        for b in range(nb):
            upper = pltpu.roll(dvec[...], (model - b * each) % model, 1)[:, :128]
            lower = pltpu.roll(heads, (width - b * each_out) % width, 1)[:, :128]
            R.gsm[b // 4, (b // 2) % 2, b % 2] = jnp.where(row < 6, upper, lower)
        push(*RS[12])
    else:
        R.g_heads[...] = heads
        R.g_vec[...] = dvec[...]
        for j in range(3):
            src = wd.at[0, 0, 0, j % 2 * each : (j % 2 + 1) * each, j // 2 * width : (j // 2 + 1) * width]
            copies.append(pltpu.make_async_copy(src, R.g_qkv.at[j * each : (j + 1) * each], misc.at[6 + j]))
            copies[-1].start()

    def input_part(i):
        val = sum(nt(d.tile(i)[...], pair_w(p)) for p, d in enumerate(d_pairs))
        s1[at(i), :] = val.astype(bf16)
        exch(3, i).start()

    each_tile(input_part, 0, mid)
    if routes:
        push(*RS[13])
    each_tile(input_part, mid, tiles)
    if routes:
        push(*RS[14])

    def finish(i):
        exch(3, i).wait()
        val = io[at(i), :].astype(f32) + (s1[at(i), :].astype(f32) + q1[at(i), :].astype(f32))
        s1[at(i), :] = val.astype(bf16)
        pltpu.make_async_copy(s1.at[at(i)], dx_hbm.at[at(i)], dx_sem.at[i]).start()

    each_tile(finish, 0, tiles)
    if routes:
        push(*RS[15])
    else:
        for cp in copies:
            cp.wait()
    each_tile(lambda i: pltpu.make_async_copy(s1.at[at(i)], dx_hbm.at[at(i)], dx_sem.at[i]).wait(), 0, tiles)


def layer(x, cot, segments, slopes, weights):
    routes = routed()
    lead = TORUS if routes else (1, 1, 1)
    rows, model = x.shape
    count, seq = segments.shape
    width, ff = weights.qkv.shape[-1], weights.gate_up.shape[-1]
    pairs, tiles = width // 128, rows // TM
    nb = lead[0] * lead[1] * lead[2]
    each, each_out, each_ff = model // nb, width // nb, ff // nb
    pad_out = -(-each_out // 32) * 32
    dma = pltpu.SemaphoreType.DMA
    low = lambda *s: (s, bf16)
    full = lambda *s: (s, f32)
    ins = [("seg", segments, VMEM), ("slope", slopes, SMEM), ("x", x, ANY), ("cot", cot, ANY)]
    outs = [("out", low(rows, model), ANY), ("dx", low(rows, model), ANY)]
    outs += [("keep", low(tiles // 2, 2, TM, 3 * width), ANY)]
    if routes:
        ins += [("weight_qkv", weights.qkv, ANY), ("weight_gate_up", weights.gate_up, ANY)]
        ins += [("weight_down", weights.down, ANY), ("weight_out", weights.out, ANY)]
        ins += [("head_bias", weights.heads, VMEM), ("norm_vectors", weights.vectors, VMEM)]
        outs += [
            ("g_qkv", full(3 * each, width), VMEM),
            ("g_gate", full(each, ff), VMEM),
            ("g_up", full(each, ff), VMEM),
            ("g_down", full(each_ff, model), VMEM),
            ("g_out", full(pad_out, model), VMEM),
            ("g_small", full(8, 128), VMEM),
        ]
    else:
        ins += [("weight_qkv", weights.qkv, ANY)]
        ins += [("weight_gate", weights.gate_up[0], ANY)]
        ins += [("weight_up", weights.gate_up[1], ANY)]
        ins += [("weight_down", weights.down, ANY), ("weight_out", weights.out, ANY)]
        ins += [("small", weights.small, ANY)]
        outs += [
            ("g_qkv", low(3 * model, width), ANY),
            ("g_gate", low(model, ff), ANY),
            ("g_up", low(model, ff), ANY),
            ("g_down", low(ff, model), ANY),
            ("g_out", low(width, model), ANY),
            ("g_heads", full(8, width), VMEM),
            ("g_vec", full(8, model), VMEM),
        ]
    scratch = [
        ("wq", low(*lead, 3 * each, width)),
        ("wg", low(*lead, each, ff)),
        ("wu", low(*lead, each, ff)),
        ("wd", low(*lead, each_ff, model)),
        ("gd", low(*lead, each_ff, model)),
        ("wo5", low(*lead, pad_out, model)),
        ("sm", low(*lead, 16, 128 if routes else model)),
        ("wo", low(width, model)),
        ("vec", full(16, model)),
        ("n1", full(rows, model)),
        ("ctx", low(rows, width)),
        ("lse", full(count * pairs, 8, seq)),
        ("vt", low(128, seq)),
        ("dvec", full(8, model)),
    ]
    scratch += [(n, low(rows, model)) for n in ("io", "s1", "q1", "s2", "q2")]
    scratch += [(n, low(tiles // 2, 2, TM, ff)) for n in ("hv", "av", "bv")]
    sems = [("io_sem", dma((tiles,))), ("out_sem", dma((tiles,))), ("dx_sem", dma((tiles,)))]
    sems += [("xs", dma((4, tiles))), ("xr", dma((4, tiles))), ("misc", dma((12,)))]
    sems += [("ready", pltpu.SemaphoreType.REGULAR((3,)))]
    if routes:
        scratch += [
            ("qkv_src", low(3 * each, width)),
            ("gate_src", low(each, ff)),
            ("up_src", low(each, ff)),
            ("down_src", low(each_ff, model)),
            ("out_src", low(pad_out, model)),
            ("small_src", low(16, 128)),
            ("spot", full(16, 128)),
            ("gsm", full(*lead, 8, 128)),
        ]
        for name, shape in (("rs", full(8, 128)),):
            for j, front in enumerate(((4, 2), (4,), (3,))):
                scratch.append((name + str(j + 1), (front + shape[0], shape[1])))
        sems += [("gs", dma((20, 5))), ("gr", dma((20, 5))), ("gl", dma((20,)))]
        sems += [("ss", dma((24, 5))), ("sr", dma((24, 5)))]
    names = [n for group in (ins, outs, scratch, sems) for n, *_ in group]
    got = pl.pallas_call(
        functools.partial(layer_kernel, names, seq, pairs, routes, lead),
        out_shape=[jax.ShapeDtypeStruct(*s) for _, s, _ in outs],
        in_specs=[space for _, _, space in ins],
        out_specs=[space for _, _, space in outs],
        scratch_shapes=[pltpu.VMEM(*s) for _, s in scratch] + [s for _, s in sems],
        compiler_params=pltpu.CompilerParams(
            vmem_limit_bytes=64 << 20, collective_id=0, has_side_effects=True
        ),
        name="layer",
    )(*[a for _, a, _ in ins])
    return types.SimpleNamespace(**{n: a for (n, *_), a in zip(outs, got)})


def adam_update(weight_old, first_old, second_old, gradient, step_rate):
    first_new = beta_first * first_old + (1.0 - beta_first) * gradient
    second_new = beta_second * second_old + (1.0 - beta_second) * gradient * gradient
    first_hat = first_new / (1.0 - beta_first**STEP)
    second_hat = second_new / (1.0 - beta_second**STEP)
    weight_new = weight_old - step_rate * (
        first_hat / (jnp.sqrt(second_hat) + adam_epsilon) + decay_rate * weight_old
    )
    return (second_new, weight_new)


def update_kernel(*refs):
    out_in, dx_in, qkv, out, gate, up, down, small = refs[:8]
    olds = [refs[8 + 3 * j : 11 + 3 * j] for j in range(6)]
    out_ref, dx_ref = refs[26:28]
    news = [refs[28 + 3 * j : 31 + 3 * j] for j in range(6)]
    hold, sem = refs[46:]
    ends = ((out_in, out_ref), (dx_in, dx_ref))
    come = [pltpu.make_async_copy(a, hold.at[j], sem.at[0, j]) for j, (a, _) in enumerate(ends)]
    leave = [pltpu.make_async_copy(hold.at[j], b, sem.at[1, j]) for j, (_, b) in enumerate(ends)]
    for cp in come:
        cp.start()

    def write(j, at, grad):
        weight, first, second = (r[at] for r in olds[j])
        rate = matrix_rate if j < 4 else vector_rate
        second_new, weight_new = adam_update(weight, first, second, grad, rate)
        for ref, val in zip(news[j], (grad, second_new, weight_new)):
            ref[at] = val

    for cp, onward in zip(come, leave):
        cp.wait()
        onward.start()
    rows = olds[0][0].shape[1]
    for j in range(3):
        cols = slice(j * 128, (j + 1) * 128)
        mine = [qkv[p * rows : (p + 1) * rows, cols] for p in range(qkv.shape[0] // rows)]
        write(0, j, jnp.concatenate(mine, axis=1))
    whole = (slice(None), slice(None))
    write(1, whole, out[: olds[1][0].shape[0], :])
    write(2, 0, gate[...])
    write(2, 1, up[...])
    write(3, whole, down[...])
    write(4, whole, small[6:8, : olds[4][0].shape[1]])
    write(5, whole, small[0:6, : olds[5][0].shape[1]])
    for cp in leave:
        cp.wait()


def update(layer_out, input_grad, sums, olds):
    flat = [a for group in olds for a in group]
    shape = lambda a: jax.ShapeDtypeStruct(a.shape, a.dtype)
    return pl.pallas_call(
        update_kernel,
        out_shape=[shape(layer_out), shape(input_grad)] + [shape(a) for a in flat],
        in_specs=[ANY] * 2 + [VMEM] * (len(sums) + len(flat)),
        out_specs=[ANY] * 2 + [VMEM] * len(flat),
        scratch_shapes=[
            pltpu.VMEM((2,) + layer_out.shape, layer_out.dtype),
            pltpu.SemaphoreType.DMA((2, 2)),
        ],
        compiler_params=pltpu.CompilerParams(vmem_limit_bytes=64 << 20),
        name="update",
    )(layer_out, input_grad, *sums, *flat)


def shards(
    inputs,
    segments,
    cotangent,
    weight_qkv,
    first_qkv,
    second_qkv,
    weight_out,
    first_out,
    second_out,
    weight_gate_up,
    first_gate_up,
    second_gate_up,
    weight_down,
    first_down,
    second_down,
    head_bias,
    first_head_bias,
    second_head_bias,
    norm_vectors,
    first_norm_vectors,
    second_norm_vectors,
):
    slopes = jnp.asarray(alibi_slopes(HEADS) * np.float32(LOG2E))
    model, width = weight_out.shape[1], weight_qkv.shape[2]
    space = types.SimpleNamespace
    olds = [
        (weight_qkv, first_qkv, second_qkv),
        (weight_out, first_out, second_out),
        (weight_gate_up, first_gate_up, second_gate_up),
        (weight_down, first_down, second_down),
        (head_bias, first_head_bias, second_head_bias),
        (norm_vectors, first_norm_vectors, second_norm_vectors),
    ]
    if routed():
        shares = space(
            qkv=weight_qkv, gate_up=weight_gate_up, down=weight_down, out=weight_out,
            heads=head_bias, vectors=norm_vectors,
        )
        got = layer(inputs, cotangent, segments, slopes, shares)
        sums = [got.g_qkv, got.g_out, got.g_gate, got.g_up, got.g_down, got.g_small]
    else:
        whole = lambda v, axis: lax.all_gather(v.astype(bf16), "dp", axis=axis, tiled=True)
        small = jnp.zeros((16, model), bf16)
        small = small.at[:6].set(whole(norm_vectors, 1)).at[6:8, :width].set(whole(head_bias, 1))
        packed = whole(weight_qkv, 1).reshape(3, model, -1, 128).transpose(2, 1, 0, 3).reshape(-1, width)
        shares = space(
            qkv=packed, gate_up=whole(weight_gate_up, 1), down=whole(weight_down, 0),
            out=whole(weight_out, 0), small=small,
        )
        got = layer(inputs, cotangent, segments, slopes, shares)
        owned = lambda v, axis: lax.psum_scatter(
            v.astype(f32), "dp", scatter_dimension=axis, tiled=True
        )
        heads, vectors = owned(got.g_heads[6:8], 1), owned(got.g_vec[:6], 1)
        small = jnp.zeros((8, 128), f32)
        small = lax.dynamic_update_slice(small, vectors, (0, 0))
        small = lax.dynamic_update_slice(small, heads, (6, 0))
        sums = [
            owned(got.g_qkv.reshape(-1, model, width), 1).reshape(-1, width),
            owned(got.g_out, 0),
            owned(got.g_gate, 0),
            owned(got.g_up, 0),
            owned(got.g_down, 0),
            small,
        ]
    return tuple(update(got.out, got.dx, sums, olds))


def solution(mesh):
    rows, both, cols = P("dp", None), P(("tensor", "dp"), None), P(None, "dp", "tensor")
    heads, vectors = P(None, ("tensor", "dp")), P(None, "dp")
    params = [s for s in (cols, both, cols, both, heads, vectors) for _ in range(3)]
    return jax.shard_map(
        shards,
        mesh=mesh,
        in_specs=(rows, rows, rows, *params),
        out_specs=(rows, rows, *params),
        check_vma=False,
    )
```

profile of v0, /device:TPU:0, one launch (start us, length us, event | category | flops | bytes accessed | tf_op | source)
XLA Modules:
  0.0 238.8 jit_solution(15711818078501652272)
XLA Ops:
  0.7 229.0 %layer.1 = (bf16[2048,768]{1,0:T(8,128)(2,1)}, bf16[2048,768]{1,0:T(8,128)(2,1)}, bf16[4,2,256,1152]{3,2,1,0:T(8,128)(2,1)}, f32[144,384]{1,0:T(8,128)}, f32[48,...) custom-call(s32[2,1024]{1,0:T(2,128)} %refs_0_.1, ...), custom_call_target="tpu_custom_call" | custom-call | tf_op jit(solution)/shard_map/layer/pallas_call | solution.py:1085
  229.6 8.9 %update.1 = (bf16[2048,768]{1,0:T(8,128)(2,1)}, bf16[2048,768]{1,0:T(8,128)(2,1)}, f32[3,48,384]{2,1,0:T(8,128)}, f32[3,48,384]{2,1,0:T(8,128)}, f32[3,48,384]{2...) custom-call(bf16[2048,768]{1,0:T(8,128)(2,1)} %get-tuple-element.28., ...), custom_call_target="tpu_custom_call" | custom-call | tf_op jit(solution)/shard_map/update/pallas_call | solution.py:1151
where the time goes:
time: 243 us; the launch traced here: 239 us
  Pallas kernels  238 us (98%)
    pallas_call x1, Pallas kernels, layer(): pl.pallas_call(functools.partial(layer_kernel, names, seq, pairs, routes,...  229 us
    pallas_call x1, Pallas kernels, update(): pl.pallas_call(update_kernel, out_shape=[shape(layer_out), shape(input_gr...  8.94 us

commit v1 on v0

--- a/solution.py
+++ b/solution.py
@@ -602,8 +602,13 @@
 
     def forward(it):
         pair, turn = lax.div(it, count), lax.rem(it, count)
-        far.fill(seg_ref, turn)
-        attend(turn, pair, *qkv, vt, far, slopes_of(pair), ctx, lse, seq, pairs)
+        s = turn + lax.rem(pair, 2) * (count - 1 - 2 * turn)
+
+        @pl.when((turn > 0) | (pair == 0))
+        def _():
+            far.fill(seg_ref, s)
+
+        attend(s, pair, *qkv, vt, far, slopes_of(pair), ctx, lse, seq, pairs)
         for p in range(pairs):
 
             @pl.when(it == p * count + count - 2)
@@ -928,9 +933,14 @@
 
     def backward(pair):
         def one(turn):
-            far.fill(seg_ref, turn)
+            s = turn + lax.rem(pair, 2) * (count - 1 - 2 * turn)
+
+            @pl.when((turn > 0) | (pair == 0))
+            def _():
+                far.fill(seg_ref, s)
+
             attend_back(
-                turn, pair, *qkv, ctx, s2, lse, far, slopes_of(pair), vt, dk_acc, dv_acc, *qkv, seq, pairs
+                s, pair, *qkv, ctx, s2, lse, far, slopes_of(pair), vt, dk_acc, dv_acc, *qkv, seq, pairs
             )
 
         each_tile(one, 0, count - 1)

time: 243 us -> 244 us (level)
  no operation moved by 1% of the time
where the time goes in v1:
time: 244 us; the launch traced here: 240 us
  Pallas kernels  239 us (98%)
    pallas_call x1, Pallas kernels, layer(): pl.pallas_call(functools.partial(layer_kernel, names, seq, pairs, routes,...  230 us
    pallas_call x1, Pallas kernels, update(): pl.pallas_call(update_kernel, out_shape=[shape(layer_out), shape(input_gr...  8.94 us

profile of v1, /device:TPU:0, one launch (start us, length us, event | category | flops | bytes accessed | tf_op | source)
XLA Modules:
  0.0 239.6 jit_solution(6034775182242264425)
XLA Ops:
  0.7 229.8 %layer.1 = (bf16[2048,768]{1,0:T(8,128)(2,1)}, bf16[2048,768]{1,0:T(8,128)(2,1)}, bf16[4,2,256,1152]{3,2,1,0:T(8,128)(2,1)}, f32[144,384]{1,0:T(8,128)}, f32[48,...) custom-call(s32[2,1024]{1,0:T(2,128)} %refs_0_.1, ...), custom_call_target="tpu_custom_call" | custom-call | tf_op jit(solution)/shard_map/layer/pallas_call | solution.py:1095
  230.4 8.9 %update.1 = (bf16[2048,768]{1,0:T(8,128)(2,1)}, bf16[2048,768]{1,0:T(8,128)(2,1)}, f32[3,48,384]{2,1,0:T(8,128)}, f32[3,48,384]{2,1,0:T(8,128)}, f32[3,48,384]{2...) custom-call(bf16[2048,768]{1,0:T(8,128)(2,1)} %get-tuple-element.28., ...), custom_call_target="tpu_custom_call" | custom-call | tf_op jit(solution)/shard_map/update/pallas_call | solution.py:1161
